TPU v7x, 256 devices: a whole 4x4x8 slice. The times are simulated.
256 devices in a mesh: blk: 64 (over x, z, core), rep: 4 (over y).
Axes of the slice: x: 4, y: 4, z: 8, core: 2. Of those that a mesh axis runs over, the one named last changes fastest.
Arguments:
- amplitudes: bfloat16 [256, 196608], P(None, ('blk', 'rep')), may hold values from -6 to 6
- panels: bfloat16 [11008, 192, 768], P(('blk', 'rep')), may hold values from -0.21875 to 0.21875
- panel_owner_index: int32 [11008, 1], P(('blk', 'rep')), may hold values from 0 to 63; in each aligned block of 43 rows (0 to 42, 43 to 85, ...) at most 2 rows name the same one
- panel_target_tile: int32 [11008], P(('blk', 'rep')), may hold values from 0 to 15
- panel_tile_mask: int32 [11008, 4], P(('blk', 'rep')), may hold values 0 or 1
- tile_sizes: int32 [1024], replicated, may hold values from 64 to 192
- tile_irreps: int32 [1024], replicated, may hold values from 0 to 1
- occ_energy: float32 [256], P('rep'), may hold values from -3 to -0.5
- vir_energy: float32 [196608], P('blk'), may hold values from 0.5 to 6
Outputs:
- doubles_update: bfloat16 [256, 196608], P('rep', 'blk')
Inputs may be any that keep to these rules, and one draw needn't show every extreme that they name: `panel_owner_index`: within the 43 rows of one device no index of blk is named more than 2 times, a bound that some block reaches.
All inputs are finite; a program needn't handle non-finite values. No bound on the sum of `panel_tile_mask` on one device may be relied on, other than what follows from the above.
Results may differ from a plain program's by a relative error of at most 0.0049.
Values may be sent and summed in bfloat16 or wider, within the bound.
A program may use at most 128 MiB of HBM per device.

v0:
```python
import jax
import jax.numpy as jnp
from jax import lax
from jax.sharding import PartitionSpec as P


def shards(
    amplitudes,
    panels,
    panel_owner_index,
    panel_target_tile,
    panel_tile_mask,
    tile_sizes,
    tile_irreps,
    occ_energy,
    vir_energy,
):
    blk_count = lax.axis_size("blk")
    rep_count = lax.axis_size("rep")
    device = lax.axis_index("blk") * rep_count + lax.axis_index("rep")
    blk_index = lax.axis_index("blk")
    slot_count, tile_width, k_columns = panels.shape
    tiles_here = k_columns // tile_width
    row_count = amplitudes.shape[0]
    owned_tiles = tiles_here * rep_count
    capacity = max(2, (2 * slot_count + blk_count - 1) // blk_count)
    in_tile = jnp.arange(tile_width, dtype=jnp.int32)
    sizes_here = lax.dynamic_slice_in_dim(tile_sizes, device * tiles_here, tiles_here, 0)
    keep_cols = (in_tile[None, :] < sizes_here[:, None]).reshape(k_columns).astype(jnp.bfloat16)
    amp_live = amplitudes * keep_cols[None, :]
    owners = panel_owner_index[:, 0]
    tile_target = owners * owned_tiles + panel_target_tile
    irrep_source = lax.dynamic_slice_in_dim(tile_irreps, device * tiles_here, tiles_here, 0)
    irrep_target = tile_irreps[tile_target]
    live_blocks = (
        panel_tile_mask * (irrep_source[None, :] == irrep_target[:, None]).astype(jnp.int32)
    ).astype(jnp.bfloat16)
    panel_live = (
        panels.reshape(slot_count, tile_width, tiles_here, tile_width)
        * live_blocks[:, None, :, None]
    ).reshape(slot_count, tile_width, k_columns)
    partial_value = jnp.einsum(
        "slk,rk->slr", panel_live, amp_live, preferred_element_type=jnp.float32
    ).astype(jnp.bfloat16)
    order = jnp.arange(slot_count, dtype=jnp.int32)
    same_owner = (owners[:, None] == owners[None, :]) & (order[:, None] > order[None, :])
    slot_rank = jnp.sum(same_owner.astype(jnp.int32), axis=1)
    position = owners * capacity + slot_rank
    outbox = (
        jnp.zeros((blk_count * capacity, tile_width, row_count), jnp.bfloat16)
        .at[position]
        .set(partial_value)
    )
    outbox_ids = (
        jnp.full((blk_count * capacity,), owned_tiles, jnp.int32)
        .at[position]
        .set(panel_target_tile)
    )
    tile_ids = lax.all_to_all(outbox_ids, "blk", split_axis=0, concat_axis=0, tiled=True)
    tile_range = jnp.arange(owned_tiles, dtype=jnp.int32)
    received = lax.all_to_all(
        lax.all_to_all(outbox, "blk", split_axis=0, concat_axis=0, tiled=True),
        "rep",
        split_axis=2,
        concat_axis=0,
        tiled=True,
    )
    all_ids = lax.all_gather(tile_ids, "rep", axis=0, tiled=True)
    onehot = (all_ids[:, None] == tile_range[None, :]).astype(jnp.bfloat16)
    summed = jnp.einsum("mt,mcr->tcr", onehot, received, preferred_element_type=jnp.float32)
    shares = summed.reshape(owned_tiles * tile_width, row_count // rep_count)
    sizes_owned = lax.dynamic_slice_in_dim(tile_sizes, blk_index * owned_tiles, owned_tiles, 0)
    keep_out = (in_tile[None, :] < sizes_owned[:, None]).reshape(owned_tiles * tile_width)
    ladder_rows = shares.T
    denominator = occ_energy[:, None] - vir_energy[None, :]
    result = jnp.where(keep_out[None, :], ladder_rows / denominator, jnp.zeros_like(ladder_rows))
    return result.astype(jnp.bfloat16)


def solution(mesh):
    return jax.shard_map(
        shards,
        mesh=mesh,
        in_specs=(
            P(None, ("blk", "rep")),
            P(("blk", "rep"), None, None),
            P(("blk", "rep"), None),
            P(("blk", "rep")),
            P(("blk", "rep"), None),
            P(),
            P(),
            P("rep"),
            P("blk"),
        ),
        out_specs=P("rep", "blk"),
        check_vma=False,
    )
```

profile of v0, /device:TPU:6, one launch (start us, length us, event | category | flops | bytes accessed | tf_op | source)
XLA Modules:
  0.0 505.0 jit_solution(4351953480227384322)
XLA Ops:
  0.0 0.7 compare_select_fusion
  0.7 0.8 dynamic_slice.10
  1.5 1.5 gather_fusion
  2.9 0.8 select_convert_fusion
  3.7 0.1 copy.27
  3.8 0.1 mul.55
  3.9 0.1 mul.56
  4.0 0.8 dynamic_slice.11
  4.8 0.1 fusion.18
  4.9 0.1 reshape.49
  5.0 0.9 convert_reduce_fusion
  5.9 0.7 fusion.19
  6.5 10.1 %fusion.6 = bf16[43,192,256]{2,1,0:T(8,128)(2,1)} fusion(bf16[43,192,768]{2,1,0:T(8,128)(2,1)} %param.10, bf16[43,768]{1,0:T(8,128)(2,1)S(1)} %mul.56, bf16[256,768]{1,0:T(8,128)(2,1)} %param.9, bf16[768]{0:T(1024)(128)(2,1)S(1)} %reshape.49), kind=kOutput, calls=%fused_computation.9 | convolution fusion | flops 3255042048 | bytes 17369088 | tf_op jit(solution)/shard_map/slk,rk->slr/dot_general | solution.py:42
  16.6 6.0 %broadcast_in_dim.15 = bf16[128,192,256]{2,1,0:T(8,128)(2,1)} broadcast(bf16[]{:T(256)} %constant.7.clone.1), dimensions={} | broadcast | bytes 12582914 | tf_op jit(solution)/shard_map/broadcast_in_dim | solution.py:50
  22.6 15.0 %scatter_fusion = bf16[128,192,256]{2,1,0:T(8,128)(2,1)} fusion(bf16[128,192,256]{2,1,0:T(8,128)(2,1)} %broadcast_in_dim.15, s32[43]{0:T(128)S(1)} %fusion.19, bf16[43,192,256]{2,1,0:T(8,128)(2,1)} %fusion.6), kind=kCustom, calls=%fused_computation.2 | custom fusion | bytes 12681388 | tf_op jit(solution)/shard_map/scatter | solution.py:52
  37.6 12.3 %all-to-all-start.1 = ((bf16[128,192,256]{2,1,0:T(8,128)(2,1)}), bf16[128,192,256]{2,1,0:T(8,128)(2,1)}, u32[]{:S(2)}, u32[]{:S(2)}) async-start(bf16[128,192,256]{2,1,0:T(8,128)(2,1)} %scatter_fusion), calls=%async_computation.1 | async-start | bytes 25165824 | tf_op jit(solution)/shard_map/all_to_all | solution.py:62
  49.9 0.8 scatter_custom_fusion
  50.8 0.8 all_to_all.24
  51.5 271.9 %all-to-all-done.1 = bf16[128,192,256]{2,1,0:T(8,128)(2,1)} async-done(((bf16[128,192,256]{2,1,0:T(8,128)(2,1)}), bf16[128,192,256]{2,1,0:T(8,128)(2,1)}, u32[]{:S(2)}, u32[]{:S(2)}) %all-to-all-start.1) | async-done | bytes 12582944 | tf_op jit(solution)/shard_map/all_to_all | solution.py:62
  323.5 8.1 %all-to-all-start = ((s32[64,2,1]{1,2,0:T(1,128)}), s32[64,2,1]{1,2,0:T(1,128)S(1)}, u32[]{:S(2)}, u32[]{:S(2)}) async-start(s32[64,2,1]{1,2,0:T(1,128)} %bitcast.3), calls=%async_computation | async-start | bytes 65536 | tf_op jit(solution)/shard_map/all_to_all | solution.py:59
  331.6 18.1 %copy.28 = bf16[128,192,256]{0,1,2:T(8,128)(2,1)} copy(bf16[128,192,256]{2,1,0:T(8,128)(2,1)} %all-to-all-done.1) | data formatting | bytes 25165824 | tf_op jit(solution)/shard_map/all_to_all | solution.py:62
  349.7 0.0 all-to-all-done
  349.7 6.3 %all-to-all-start.2 = ((bf16[128,192,256]{0,1,2:T(8,128)(2,1)}), bf16[128,192,256]{0,1,2:T(8,128)(2,1)}, u32[]{:S(2)}, u32[]{:S(2)}) async-start(bf16[128,192,256]{0,1,2:T(8,128)(2,1)} %copy.28), calls=%async_computation.2 | async-start | bytes 25165824 | tf_op jit(solution)/shard_map/all_to_all | solution.py:61
  356.0 0.0 copy-start
  356.0 0.0 copy-start.1
  356.0 0.8 dynamic_slice.9
  356.8 0.1 iota_compare_fusion.2
  356.9 0.1 lt.58
  357.0 0.5 broadcast.45
  357.5 0.7 reduce.3
  358.2 0.1 reshape.75
  358.4 138.9 %all-gather = s32[4,1,128]{2,1,0:T(1,128)S(1)} all-gather(s32[1,1,128]{2,1,0:T(1,128)S(1)} %reshape.75), channel_id=1, replica_groups=mesh['blk'=64,'rep'=4] {'rep'}, dimensions={0}, use_global_device_ids=true | all-gather | bytes 2560 | tf_op jit(solution)/shard_map/all_gather | solution.py:68
  497.3 0.0 all-to-all-done.2
  497.3 6.3 %fusion.2 = f32[16,192,64]{1,0,2:T(8,128)S(1)} fusion(bf16[4,64,24,8,128]{4,3,2,1,0:T(8,128)(2,1)} %bitcast.11, s32[512]{0:T(512)S(1)} %bitcast.32), kind=kOutput, calls=%fused_computation.5 | convolution fusion | flops 201334784 | bytes 13371392 | tf_op jit(solution)/shard_map/mt,mcr->tcr/dot_general | solution.py:70
  503.6 0.4 reshape.48
  504.1 0.0 copy-done
  504.1 0.0 copy-done.1
  504.1 0.9 fusion.10
  (1 shorter events, 0.0 us)
Async XLA Ops:
  37.6 285.9 %all-to-all-start.1 = ((bf16[128,192,256]{2,1,0:T(8,128)(2,1)}), bf16[128,192,256]{2,1,0:T(8,128)(2,1)}, u32[]{:S(2)}, u32[]{:S(2)}) async-start(bf16[128,192,256]{2,1,0:T(8,128)(2,1)} %scatter_fusion), calls=%async_computation.1 | async-start | bytes 25165824 | tf_op jit(solution)/shard_map/all_to_all | solution.py:62
  323.5 26.2 %all-to-all-start = ((s32[64,2,1]{1,2,0:T(1,128)}), s32[64,2,1]{1,2,0:T(1,128)S(1)}, u32[]{:S(2)}, u32[]{:S(2)}) async-start(s32[64,2,1]{1,2,0:T(1,128)} %bitcast.3), calls=%async_computation | async-start | bytes 65536 | tf_op jit(solution)/shard_map/all_to_all | solution.py:59
  349.7 147.6 %all-to-all-start.2 = ((bf16[128,192,256]{0,1,2:T(8,128)(2,1)}), bf16[128,192,256]{0,1,2:T(8,128)(2,1)}, u32[]{:S(2)}, u32[]{:S(2)}) async-start(bf16[128,192,256]{0,1,2:T(8,128)(2,1)} %copy.28), calls=%async_computation.2 | async-start | bytes 25165824 | tf_op jit(solution)/shard_map/all_to_all | solution.py:61
  356.0 148.0 %copy-start = (f32[3072]{0:T(1024)S(1)}, f32[3072]{0:T(1024)}, u32[]{:S(2)}) copy-start(f32[3072]{0:T(1024)} %param.17) | copy-start | bytes 36868
  356.0 148.0 %copy-start.1 = (f32[64]{0:T(128)S(1)}, f32[64]{0:T(128)}, u32[]{:S(2)}) copy-start(f32[64]{0:T(128)} %param.16) | copy-start | bytes 772
where the time goes:
time: 506 us; the launch traced here: 505 us
  waiting for transfers between devices  272 us (54%)
  blocking collectives  139 us (27%)
  local copies, waits for them, and re-layouts  46 us (9%)
  starting transfers between devices  26.8 us (5%)
  matrix products  16.4 us (3%)
    all_to_all x1, waiting for transfers between devices, shards(): lax.all_to_all(outbox, 'blk', split_axis=0, concat_axis=0, tiled=True)  272 us
    all_gather x1, blocking collectives, shards(): all_ids = lax.all_gather(tile_ids, 'rep', axis=0, tiled=True)  139 us
    all_to_all x1, local copies, waits for them, and re-layouts, shards(): lax.all_to_all(outbox, 'blk', split_axis=0, concat_axis=0, tiled=True)  18.1 us
    scatter x1, local copies, waits for them, and re-layouts, shards(): outbox = jnp.zeros((blk_count * capacity, tile_width, row_count), jnp.bfl...  15 us
    all_to_all x1, starting transfers between devices, shards(): lax.all_to_all(outbox, 'blk', split_axis=0, concat_axis=0, tiled=True)  12.3 us
  transfers between devices with their start and end apart: 3, of which 1 were waited for; matrix products, arithmetic and copies ran while one was open for 4% of the time, Pallas kernels for 0%

commit v1 on v0

--- a/solution.py
+++ b/solution.py
@@ -65,7 +65,12 @@
         concat_axis=0,
         tiled=True,
     )
-    all_ids = lax.all_gather(tile_ids, "rep", axis=0, tiled=True)
+    ring = [tile_ids]
+    for hop in range(3):
+        ring.append(lax.ppermute(ring[-1], "rep", [(dev, (dev + 1) % 4) for dev in range(4)]))
+    all_ids = jnp.roll(
+        jnp.concatenate(ring[::-1], axis=0), (lax.axis_index("rep") + 1) * ring[0].shape[0], axis=0
+    )
     onehot = (all_ids[:, None] == tile_range[None, :]).astype(jnp.bfloat16)
     summed = jnp.einsum("mt,mcr->tcr", onehot, received, preferred_element_type=jnp.float32)
     shares = summed.reshape(owned_tiles * tile_width, row_count // rep_count)

time: 506 us -> 511 us (level)
  blocking collectives: 139 us -> 0 us
  waiting for transfers between devices: 272 us -> 411 us
    ppermute x0 -> x3, waiting for transfers between devices: none -> 139 us  [shards(): lax.ppermute(ring[-1], 'rep', [(dev, (dev + 1) % 4) for dev in range(4)])]
    all_gather x1 -> x0, blocking collectives: 139 us -> none  [shards(): all_ids = lax.all_gather(tile_ids, 'rep', axis=0, tiled=True)]
  transfers between devices with their start and end apart: 3 -> 6, of which waited for: 1 -> 4; matrix products, arithmetic and copies ran while one was open for 4% -> 4% of each run, Pallas kernels for 0% -> 0%
where the time goes in v1:
time: 511 us; the launch traced here: 510 us
  waiting for transfers between devices  411 us (80%)
  local copies, waits for them, and re-layouts  46.2 us (9%)
  starting transfers between devices  31.6 us (6%)
  matrix products  16.4 us (3%)
    all_to_all x1, waiting for transfers between devices, shards(): lax.all_to_all(outbox, 'blk', split_axis=0, concat_axis=0, tiled=True)  272 us
    ppermute x3, waiting for transfers between devices, shards(): lax.ppermute(ring[-1], 'rep', [(dev, (dev + 1) % 4) for dev in range(4)])  139 us
    all_to_all x1, local copies, waits for them, and re-layouts, shards(): lax.all_to_all(outbox, 'blk', split_axis=0, concat_axis=0, tiled=True)  18.2 us
    scatter x1, local copies, waits for them, and re-layouts, shards(): outbox = jnp.zeros((blk_count * capacity, tile_width, row_count), jnp.bfl...  14.9 us
    all_to_all x1, starting transfers between devices, shards(): lax.all_to_all(outbox, 'blk', split_axis=0, concat_axis=0, tiled=True)  12.5 us
  transfers between devices with their start and end apart: 6, of which 4 were waited for; matrix products, arithmetic and copies ran while one was open for 4% of the time, Pallas kernels for 0%

profile of v1, /device:TPU:6, one launch (start us, length us, event | category | flops | bytes accessed | tf_op | source)
XLA Modules:
  0.0 510.1 jit_solution(12938437804131250799)
XLA Ops:
  0.0 0.9 convert_reduce_fusion
  0.9 0.7 fusion.19
  1.6 0.7 compare_select_fusion
  2.3 1.5 gather_fusion
  3.7 0.8 dynamic_slice.15
  4.5 0.8 select_convert_fusion
  5.2 0.1 copy.27
  5.4 0.1 mul.59
  5.5 0.1 mul.60
  5.6 0.8 dynamic_slice.16
  6.4 0.1 fusion.18
  6.5 0.1 reshape.49
  6.5 10.1 %fusion.6 = bf16[43,192,256]{2,1,0:T(8,128)(2,1)} fusion(bf16[43,192,768]{2,1,0:T(8,128)(2,1)} %param.10, bf16[43,768]{1,0:T(8,128)(2,1)S(1)} %mul.60, bf16[256,768]{1,0:T(8,128)(2,1)} %param.9, bf16[768]{0:T(1024)(128)(2,1)S(1)} %reshape.49), kind=kOutput, calls=%fused_computation.9 | convolution fusion | flops 3255042048 | bytes 17369088 | tf_op jit(solution)/shard_map/slk,rk->slr/dot_general | solution.py:42
  16.6 6.0 %broadcast_in_dim.15 = bf16[128,192,256]{2,1,0:T(8,128)(2,1)} broadcast(bf16[]{:T(256)} %constant.51.clone.1), dimensions={} | broadcast | bytes 12582914 | tf_op jit(solution)/shard_map/broadcast_in_dim | solution.py:50
  22.6 14.9 %scatter_fusion = bf16[128,192,256]{2,1,0:T(8,128)(2,1)} fusion(bf16[128,192,256]{2,1,0:T(8,128)(2,1)} %broadcast_in_dim.15, s32[43]{0:T(128)S(1)} %fusion.19, bf16[43,192,256]{2,1,0:T(8,128)(2,1)} %fusion.6), kind=kCustom, calls=%fused_computation.2 | custom fusion | bytes 12681388 | tf_op jit(solution)/shard_map/scatter | solution.py:52
  37.6 12.5 %all-to-all-start.1 = ((bf16[128,192,256]{2,1,0:T(8,128)(2,1)}), bf16[128,192,256]{2,1,0:T(8,128)(2,1)}, u32[]{:S(2)}, u32[]{:S(2)}) async-start(bf16[128,192,256]{2,1,0:T(8,128)(2,1)} %scatter_fusion), calls=%async_computation.1 | async-start | bytes 25165824 | tf_op jit(solution)/shard_map/all_to_all | solution.py:62
  50.1 0.8 scatter_custom_fusion
  50.9 0.8 all_to_all.24
  51.7 271.9 %all-to-all-done.1 = bf16[128,192,256]{2,1,0:T(8,128)(2,1)} async-done(((bf16[128,192,256]{2,1,0:T(8,128)(2,1)}), bf16[128,192,256]{2,1,0:T(8,128)(2,1)}, u32[]{:S(2)}, u32[]{:S(2)}) %all-to-all-start.1) | async-done | bytes 12582944 | tf_op jit(solution)/shard_map/all_to_all | solution.py:62
  323.6 8.1 %all-to-all-start = ((s32[64,2,1]{1,2,0:T(1,128)}), s32[64,2,1]{1,2,0:T(1,128)S(1)}, u32[]{:S(2)}, u32[]{:S(2)}) async-start(s32[64,2,1]{1,2,0:T(1,128)} %bitcast.3), calls=%async_computation | async-start | bytes 65536 | tf_op jit(solution)/shard_map/all_to_all | solution.py:59
  331.7 18.2 %copy.28 = bf16[128,192,256]{0,1,2:T(8,128)(2,1)} copy(bf16[128,192,256]{2,1,0:T(8,128)(2,1)} %all-to-all-done.1) | data formatting | bytes 25165824 | tf_op jit(solution)/shard_map/all_to_all | solution.py:62
  349.9 0.0 all-to-all-done
  349.9 6.3 %all-to-all-start.2 = ((bf16[128,192,256]{0,1,2:T(8,128)(2,1)}), bf16[128,192,256]{0,1,2:T(8,128)(2,1)}, u32[]{:S(2)}, u32[]{:S(2)}) async-start(bf16[128,192,256]{0,1,2:T(8,128)(2,1)} %copy.28), calls=%async_computation.2 | async-start | bytes 25165824 | tf_op jit(solution)/shard_map/all_to_all | solution.py:61
  356.2 0.0 copy-start
  356.2 0.0 copy-start.1
  356.2 0.8 dynamic_slice.13
  357.0 0.5 broadcast.46
  357.5 0.7 reduce.3
  358.3 0.1 all_to_all.26
  358.4 2.0 collective-permute-start
  360.4 0.1 iota_compare_fusion.2
  360.5 131.4 %collective-permute-done = s32[128]{0:T(128)S(1)} collective-permute-done((s32[128]{0:T(128)S(1)}, s32[128]{0:T(128)S(1)}, u32[]{:S(2)}, u32[]{:S(2)}) %collective-permute-start) | collective-permute-done | bytes 544 | tf_op jit(solution)/shard_map/ppermute | solution.py:70
  491.9 2.4 collective-permute-start.1
  494.3 3.2 collective-permute-done.1
  497.5 0.3 collective-permute-start.2
  497.8 0.1 lt.70
  497.9 4.4 collective-permute-done.2
  502.4 0.1 dynamic_slice.14
  502.4 0.0 all-to-all-done.2
  502.4 6.3 %fusion.2 = f32[16,192,64]{1,0,2:T(8,128)S(1)} fusion(bf16[4,64,24,8,128]{4,3,2,1,0:T(8,128)(2,1)} %bitcast.10, s32[512]{0:T(512)S(1)} %dynamic_slice.14), kind=kOutput, calls=%fused_computation.5 | convolution fusion | flops 201334784 | bytes 13371392 | tf_op jit(solution)/shard_map/mt,mcr->tcr/dot_general | solution.py:75
  508.8 0.4 reshape.48
  509.2 0.0 copy-done
  509.2 0.0 copy-done.1
  509.2 0.9 fusion.10
  (10 shorter events, 0.1 us)
Async XLA Ops:
  37.6 286.0 %all-to-all-start.1 = ((bf16[128,192,256]{2,1,0:T(8,128)(2,1)}), bf16[128,192,256]{2,1,0:T(8,128)(2,1)}, u32[]{:S(2)}, u32[]{:S(2)}) async-start(bf16[128,192,256]{2,1,0:T(8,128)(2,1)} %scatter_fusion), calls=%async_computation.1 | async-start | bytes 25165824 | tf_op jit(solution)/shard_map/all_to_all | solution.py:62
  323.6 26.3 %all-to-all-start = ((s32[64,2,1]{1,2,0:T(1,128)}), s32[64,2,1]{1,2,0:T(1,128)S(1)}, u32[]{:S(2)}, u32[]{:S(2)}) async-start(s32[64,2,1]{1,2,0:T(1,128)} %bitcast.3), calls=%async_computation | async-start | bytes 65536 | tf_op jit(solution)/shard_map/all_to_all | solution.py:59
  349.9 152.6 %all-to-all-start.2 = ((bf16[128,192,256]{0,1,2:T(8,128)(2,1)}), bf16[128,192,256]{0,1,2:T(8,128)(2,1)}, u32[]{:S(2)}, u32[]{:S(2)}) async-start(bf16[128,192,256]{0,1,2:T(8,128)(2,1)} %copy.28), calls=%async_computation.2 | async-start | bytes 25165824 | tf_op jit(solution)/shard_map/all_to_all | solution.py:61
  356.2 153.0 %copy-start = (f32[3072]{0:T(1024)S(1)}, f32[3072]{0:T(1024)}, u32[]{:S(2)}) copy-start(f32[3072]{0:T(1024)} %param.17) | copy-start | bytes 36868
  356.2 153.0 %copy-start.1 = (f32[64]{0:T(128)S(1)}, f32[64]{0:T(128)}, u32[]{:S(2)}) copy-start(f32[64]{0:T(128)} %param.16) | copy-start | bytes 772
  358.4 133.5 %collective-permute-start = (s32[128]{0:T(128)S(1)}, s32[128]{0:T(128)S(1)}, u32[]{:S(2)}, u32[]{:S(2)}) collective-permute-start(s32[128]{0:T(128)S(1)} %all_to_all.26), channel_id=1, source_target_pairs={{0,1},{1,2},{2,3},{3,0},{4,5},{5,6},{6,7},{7,4},{8,9},{9,10},{10,1... | collective-permute-start | bytes 1544 | tf_op jit(solution)/shard_map/ppermute | solution.py:70
  491.9 5.6 %collective-permute-start.1 = (s32[128]{0:T(128)S(1)}, s32[128]{0:T(128)S(1)}, u32[]{:S(2)}, u32[]{:S(2)}) collective-permute-start(s32[128]{0:T(128)S(1)} %collective-permute-done), channel_id=1, source_target_pairs={{0,1},{1,2},{2,3},{3,0},{4,5},{5,6},{6,7},{7,4},{8,9},{9,10},{10,1... | collective-permute-start | bytes 1544 | tf_op jit(solution)/shard_map/ppermute | solution.py:70
  497.5 4.8 collective-permute-start.2
